TPU v7x, 256 devices: a whole 4x4x8 slice. The times are simulated.
256 devices in a mesh: tup: 32 (over z, y), lang: 8 (over x, core).
Axes of the slice: x: 4, y: 4, z: 8, core: 2. Of those that a mesh axis runs over, the one named last changes fastest.
Arguments:
- counts: bfloat16 [8, 4096, 16384], P('lang', 'tup'), may hold values from 0 to 80
- lengths: int32 [8, 4096], P('lang', 'tup'), may hold values from 96 to 128, as said below
- tuple_map: int32 [8, 4096], P('lang', 'tup'), may hold values from 0 to 4095, as said below
- topic_mix: bfloat16 [4096, 256], P('tup'), may hold values from 0.049804688 to 5
- word_probs: bfloat16 [8, 16384, 256], P('lang', 'tup'), may hold values from 0.099609375 to 10
Outputs:
- mix_update: float32 [4096, 256], P('tup')
- word_update: float32 [8, 16384, 256], P('lang', 'tup')
Inputs may be any that keep to these rules, and one draw needn't show every extreme that they name: `lengths`: the first row of every language spans all 128 tiles. `tuple_map`: each language names every tuple once; the 128 rows of one index of tup hold exactly 4 tuples t of each value of t // 128.
All inputs are finite; a program needn't handle non-finite values.
Results may differ from a plain program's by a relative error of at most 0.0003.
Values may be sent and summed in bfloat16 or wider, within the bound.
No kernel may reach another device: no remote copies, remote signals or barrier semaphores. Data moves between devices by JAX's collectives and lax.ppermute only.
A program may use at most 128 MiB of HBM per device.

v0:
```python
import math
import jax
import jax.numpy as jnp
from jax import lax
from jax.sharding import PartitionSpec as P


def ratio_block(count_block, mix_block, word_block):
    expected = lax.dot_general(
        mix_block, word_block, (((1,), (1,)), ((), ())), preferred_element_type=jnp.float32
    )
    return count_block.astype(jnp.float32) / expected


def topic_term(ratios, word_block):
    return jnp.dot(ratios, word_block.astype(jnp.float32), precision=lax.Precision.HIGHEST)


def word_term(ratios, mix_rows):
    return lax.dot_general(
        ratios,
        mix_rows.astype(jnp.float32),
        (((0,), (0,)), ((), ())),
        precision=lax.Precision.HIGHEST,
    )


def ratio_pass(row_counts, mix_rows, word_local):
    shard_len = word_local.shape[0]
    topics = word_local.shape[1]
    vocab_size = shard_len * lax.axis_size("tup")
    topic_zero = jnp.zeros((row_counts.shape[0], topics), jnp.float32)
    shard_rows = lax.all_gather(word_local, "tup", axis=0, tiled=True)
    row_span = shard_rows.shape[0]
    block_len = math.gcd(row_span, 2048)

    def block_step(block_index, inner_pair):
        topic_sum, word_sum = inner_pair
        begin_row = block_index * block_len
        word_block = lax.dynamic_slice_in_dim(shard_rows, begin_row, block_len, 0)
        count_block = lax.dynamic_slice_in_dim(row_counts, begin_row, block_len, 1)
        ratios = ratio_block(count_block, mix_rows, word_block)
        topic_sum = topic_sum + topic_term(ratios, word_block)
        word_sum = lax.dynamic_update_slice_in_dim(
            word_sum, word_term(ratios, mix_rows), begin_row, 0
        )
        return (topic_sum, word_sum)

    topic_sum, word_sum = lax.fori_loop(
        0,
        row_span // block_len,
        block_step,
        (topic_zero, jnp.zeros((vocab_size, topics), jnp.float32)),
    )
    return (topic_sum, lax.psum_scatter(word_sum, "tup", scatter_dimension=0, tiled=True))


def on_device(counts, lengths, tuple_map, topic_mix, word_probs):
    count_rows = counts[0]
    tup_rows, vocab_size = count_rows.shape
    topics = topic_mix.shape[1]
    groups = lax.axis_size("tup")
    per_owner = tup_rows // groups
    tile_of = jnp.arange(vocab_size, dtype=jnp.int32) // 128
    live_counts = count_rows * (tile_of[None, :] < lengths[0][:, None]).astype(jnp.bfloat16)
    tuple_ids = tuple_map[0]
    word_local = word_probs[0]
    bucket_order = jnp.argsort(tuple_ids // tup_rows, stable=True)
    bucket_ids = tuple_ids[bucket_order].reshape(groups, per_owner)
    arrived = lax.all_to_all(
        live_counts[bucket_order].reshape(groups, per_owner, vocab_size),
        "tup",
        split_axis=0,
        concat_axis=0,
        tiled=True,
    ).reshape(tup_rows, vocab_size)
    arrived_ids = lax.all_to_all(
        bucket_ids, "tup", split_axis=0, concat_axis=0, tiled=True
    ).reshape(tup_rows)
    local_ids = arrived_ids % tup_rows
    mix_rows = topic_mix[local_ids]
    topic_sum, word_sum = ratio_pass(arrived, mix_rows, word_local)
    placed = jnp.zeros_like(topic_sum).at[local_ids].set(topic_sum)
    totals = lax.psum(placed, "lang")
    mixed = topic_mix.astype(jnp.float32) * totals
    mix_update = topics * mixed / jnp.sum(mixed, 1, keepdims=True)
    scaled = word_local.astype(jnp.float32) * word_sum
    column = lax.psum(jnp.sum(scaled, 0), "tup")
    word_update = (vocab_size * scaled / column[None, :])[None]
    return (mix_update, word_update)


def solution(mesh):
    return jax.shard_map(
        on_device,
        mesh=mesh,
        in_specs=(
            P("lang", "tup", None),
            P("lang", "tup"),
            P("lang", "tup"),
            P("tup", None),
            P("lang", "tup", None),
        ),
        out_specs=(P("tup", None), P("lang", "tup", None)),
        check_vma=False,
    )
```

profile of v0, /device:TPU:4, one launch (start us, length us, event | category | flops | bytes accessed | tf_op | source)
XLA Modules:
  0.0 659.9 jit_solution(987465419086488916)
XLA Ops:
  8.6 2.5 sort.17
  13.4 11.5 %all-to-all-start = ((s32[32,1,4]{2,1,0:T(1,128)}), s32[32,1,4]{2,1,0:T(1,128)S(1)}, u32[]{:S(2)}, u32[]{:S(2)}) async-start(s32[32,1,4]{2,1,0:T(1,128)} %bitcast.1), calls=%async_computation | async-start | bytes 32768 | tf_op jit(solution)/shard_map/all_to_all | solution.py:77
  24.9 5.4 compare_select_fusion
  30.3 11.5 %gather_fusion.1 = bf16[128,16384]{1,0:T(8,128)(2,1)} fusion(bf16[128,16384]{1,0:T(8,128)(2,1)} %compare_select_fusion, s32[1024]{0:T(1024)S(1)} %pad_clamp_fusion.1), kind=kCustom, calls=%fused_computation.1 | custom fusion | bytes 8389120 | tf_op jit(solution)/shard_map/gather | solution.py:71
  41.8 7.2 %reshape.96 = bf16[32,4,16384]{2,1,0:T(4,128)(2,1)} reshape(bf16[128,16384]{1,0:T(8,128)(2,1)} %gather_fusion.1) | data formatting | bytes 8388608 | tf_op jit(solution)/shard_map/reshape | solution.py:71
  49.1 10.0 %all-to-all-start.1 = ((bf16[32,4,16384]{2,1,0:T(4,128)(2,1)}), bf16[32,4,16384]{2,1,0:T(4,128)(2,1)}, u32[]{:S(2)}, u32[]{:S(2)}) async-start(bf16[32,4,16384]{2,1,0:T(4,128)(2,1)} %reshape.96), calls=%async_computation.1 | async-start | bytes 8388608 | tf_op jit(solution)/shard_map/all_to_all | solution.py:70
  61.6 130.7 %all-to-all-done.1 = bf16[32,4,16384]{2,1,0:T(4,128)(2,1)} async-done(((bf16[32,4,16384]{2,1,0:T(4,128)(2,1)}), bf16[32,4,16384]{2,1,0:T(4,128)(2,1)}, u32[]{:S(2)}, u32[]{:S(2)}) %all-to-all-start.1) | async-done | bytes 4194336 | tf_op jit(solution)/shard_map/all_to_all | solution.py:70
  192.2 6.9 %reshape.97 = bf16[128,16384]{1,0:T(8,128)(2,1)} reshape(bf16[32,4,16384]{2,1,0:T(4,128)(2,1)} %all-to-all-done.1) | data formatting | bytes 8388608 | tf_op jit(solution)/shard_map/reshape | solution.py:76
  199.2 6.0 broadcast_in_dim.7
  205.2 60.9 %while.16 = (s32[]{:T(128)}, f32[128,256]{1,0:T(8,128)S(1)}, f32[16384,256]{1,0:T(8,128)}, bf16[128,16384]{1,0:T(8,128)(2,1)}, bf16[16384,256]{1,0:T(8,128)(2,1)...) while((s32[]{:T(128)}, f32[128,256]{1,0:T(8,128)S(1)}, ...), condition=%wide.region_2.3_spmd.clone, body=%wide.region_1.2_spmd.clone.sunk | while | flops 1745420288 | bytes 10354869 | solution.py:49
  208.2 2.3 convolution_add_fusion.2
  210.4 2.3 convolution_dynamic-update-slice_fusion.2
  215.8 2.3 convolution_add_fusion.2
  218.1 2.3 convolution_dynamic-update-slice_fusion.2
  223.4 2.3 convolution_add_fusion.2
  225.6 2.3 convolution_dynamic-update-slice_fusion.2
  229.3 1.7 fusion.31
  231.0 2.3 convolution_add_fusion.2
  233.2 2.3 convolution_dynamic-update-slice_fusion.2
  236.9 1.7 fusion.31
  238.6 2.3 convolution_add_fusion.2
  240.9 2.4 convolution_dynamic-update-slice_fusion.2
  246.3 2.3 convolution_add_fusion.2
  248.5 2.3 convolution_dynamic-update-slice_fusion.2
  253.8 2.3 convolution_add_fusion.2
  256.1 2.3 convolution_dynamic-update-slice_fusion.2
  261.5 2.3 convolution_add_fusion.2
  263.7 2.3 convolution_dynamic-update-slice_fusion.2
  268.4 57.4 %all-reduce.2.cloned.1.call-done = f32[128,256]{1,0:T(8,128)} async-done(((f32[128,256]{1,0:T(8,128)}), f32[128,256]{1,0:T(8,128)}) %all-reduce.2.cloned.1.call-update) | async-done | bytes 131088 | tf_op jit(solution)/shard_map/psum | solution.py:84
  328.5 249.4 %reduce-scatter.2.cloned.1.call-done = f32[512,256]{1,0:T(8,128)} async-done(((f32[16384,256]{1,0:T(8,128)}), f32[512,256]{1,0:T(8,128)}) %reduce-scatter.2.cloned.1.call-update) | async-done | bytes 524304 | tf_op jit(solution)/shard_map/reduce_scatter | solution.py:55
  579.1 72.4 %psum.15 = f32[256]{0:T(256)S(1)} all-reduce(f32[256]{0:T(256)S(1)} %fusion.5), channel_id=1, replica_groups=mesh['tup'=32,'lang'=8] {'tup'}, use_global_device_ids=true, to_apply=%region_8.9 | all-reduce | flops 256 | bytes 2048 | tf_op jit(solution)/shard_map/psum | solution.py:88
  651.5 1.9 divide_bitcast_fusion
  (52 shorter events, 33.0 us)
Async XLA Ops:
  7.2 192.0 %all-gather.3.cloned.1.call-start = ((), (), s32[]{:S(2)}) async-start(), calls=%async_computation.5 | async-start | bytes 8650752 | tf_op jit(solution)/shard_map/all_gather | solution.py:33
  13.4 35.6 %all-to-all-start = ((s32[32,1,4]{2,1,0:T(1,128)}), s32[32,1,4]{2,1,0:T(1,128)S(1)}, u32[]{:S(2)}, u32[]{:S(2)}) async-start(s32[32,1,4]{2,1,0:T(1,128)} %bitcast.1), calls=%async_computation | async-start | bytes 32768 | tf_op jit(solution)/shard_map/all_to_all | solution.py:77
  49.1 11.6 %copy-start = (bf16[128,256]{1,0:T(8,128)(2,1)S(1)}, bf16[128,256]{1,0:T(8,128)(2,1)}, u32[]{:S(2)}) copy-start(bf16[128,256]{1,0:T(8,128)(2,1)} %param.10) | copy-start | bytes 196612
  49.1 143.2 %all-to-all-start.1 = ((bf16[32,4,16384]{2,1,0:T(4,128)(2,1)}), bf16[32,4,16384]{2,1,0:T(4,128)(2,1)}, u32[]{:S(2)}, u32[]{:S(2)}) async-start(bf16[32,4,16384]{2,1,0:T(4,128)(2,1)} %reshape.96), calls=%async_computation.1 | async-start | bytes 8388608 | tf_op jit(solution)/shard_map/all_to_all | solution.py:70
  59.1 266.7 %all-reduce.2.cloned.1.call-start = ((), (), s32[]{:S(2)}) async-start(), calls=%async_computation.3 | async-start | bytes 262144 | tf_op jit(solution)/shard_map/psum | solution.py:84
  267.7 310.2 %reduce-scatter.2.cloned.1.call-start = ((), (), s32[]{:S(2)}) async-start(), calls=%async_computation.4 | async-start | bytes 17301504 | tf_op jit(solution)/shard_map/reduce_scatter | solution.py:55
  267.7 310.2 %copy-start.1 = (bf16[1,512,256]{2,1,0:T(8,128)(2,1)S(1)}, bf16[1,512,256]{2,1,0:T(8,128)(2,1)}, u32[]{:S(2)}) copy-start(bf16[1,512,256]{2,1,0:T(8,128)(2,1)} %param.11) | copy-start | bytes 786436
Sparse Core Ops, SparseCore 0:
  10.6 176.9 all-gather.2
  267.8 57.9 all-reduce.1
  330.5 247.3 reduce-scatter.1
where the time goes:
time: 662 us; the launch traced here: 660 us
  waiting for transfers between devices  439 us (66%)
  blocking collectives  72.4 us (11%)
  matrix products  49.9 us (8%)
  local copies, waits for them, and re-layouts  47.8 us (7%)
  starting transfers between devices  21.8 us (3%)
  other arithmetic  15.1 us (2%)
  between operations  13.8 us (2%)
    reduce_scatter x1, waiting for transfers between devices, ratio_pass(): lax.psum_scatter(word_sum, 'tup', scatter_dimension=0, tiled=True)  249 us
    all_to_all x1, waiting for transfers between devices, on_device(): lax.all_to_all(live_counts[bucket_order].reshape(groups, per_owner, vocab...  131 us
    psum x1, blocking collectives, on_device(): column = lax.psum(jnp.sum(scaled, 0), 'tup')  72.4 us
    psum x1, waiting for transfers between devices, on_device(): totals = lax.psum(placed, 'lang')  57.4 us
    dot_general x8, matrix products, word_term(): lax.dot_general(ratios, mix_rows.astype(jnp.float32), (((0,), (0,)), ((),...  18.6 us
    dot_general x8, matrix products, topic_term(): jnp.dot(ratios, word_block.astype(jnp.float32), precision=lax.Precision.H...  18 us
    dot_general x8, matrix products, ratio_block(): lax.dot_general(mix_block, word_block, (((1,), (1,)), ((), ())), preferre...  13.3 us
  transfers between devices with their start and end apart: 5, of which 3 were waited for; matrix products, arithmetic and copies ran while one was open for 6% of the time, Pallas kernels for 0%

commit v1 on v0

--- a/solution.py
+++ b/solution.py
@@ -1,8 +1,24 @@
+import functools
 import math
 import jax
 import jax.numpy as jnp
 from jax import lax
 from jax.sharding import PartitionSpec as P
+
+
+def time_pools_over_axis(chunk, comm_axis):
+    axis_len = jax.lax.axis_size(comm_axis)
+    extra, frame_out = (chunk, 0)
+    while 1 << frame_out < axis_len:
+        carry_in = jax.lax.ppermute(
+            extra, comm_axis, list(map(lambda nth: (nth, nth ^ 1 << frame_out), range(axis_len)))
+        )
+        extra = extra + carry_in
+        frame_out = frame_out + 1
+    return extra
+
+
+entries_state = functools.partial(time_pools_over_axis, comm_axis="lang")
 
 
 def ratio_block(count_block, mix_block, word_block):
@@ -81,7 +97,7 @@
     mix_rows = topic_mix[local_ids]
     topic_sum, word_sum = ratio_pass(arrived, mix_rows, word_local)
     placed = jnp.zeros_like(topic_sum).at[local_ids].set(topic_sum)
-    totals = lax.psum(placed, "lang")
+    totals = entries_state(placed)
     mixed = topic_mix.astype(jnp.float32) * totals
     mix_update = topics * mixed / jnp.sum(mixed, 1, keepdims=True)
     scaled = word_local.astype(jnp.float32) * word_sum

time: 662 us -> 592 us (0.89)
  waiting for transfers between devices: 439 us -> 370 us
    psum x1 -> x0, waiting for transfers between devices: 57.4 us -> none  [on_device(): totals = lax.psum(placed, 'lang')]
    reduce_scatter x1, waiting for transfers between devices: 249 us -> 227 us  [ratio_pass(): lax.psum_scatter(word_sum, 'tup', scatter_dimension=0, tiled=True)]
    ppermute x0 -> x3, waiting for transfers between devices: none -> 11.6 us  [time_pools_over_axis(): jax.lax.ppermute(extra, comm_axis, list(map(lambda nth: (nth, nth ^ 1 <<...]
  transfers between devices with their start and end apart: 5 -> 7, of which waited for: 3 -> 5; matrix products, arithmetic and copies ran while one was open for 6% -> 7% of each run, Pallas kernels for 0% -> 0%
where the time goes in v1:
time: 592 us; the launch traced here: 590 us
  waiting for transfers between devices  370 us (62%)
  blocking collectives  72.2 us (12%)
  matrix products  49.9 us (8%)
  local copies, waits for them, and re-layouts  47.2 us (8%)
  starting transfers between devices  23.8 us (4%)
  between operations  14.1 us (2%)
  other arithmetic  13.3 us (2%)
    reduce_scatter x1, waiting for transfers between devices, ratio_pass(): lax.psum_scatter(word_sum, 'tup', scatter_dimension=0, tiled=True)  227 us
    all_to_all x1, waiting for transfers between devices, on_device(): lax.all_to_all(live_counts[bucket_order].reshape(groups, per_owner, vocab...  131 us
    psum x1, blocking collectives, on_device(): column = lax.psum(jnp.sum(scaled, 0), 'tup')  72.2 us
    dot_general x8, matrix products, word_term(): lax.dot_general(ratios, mix_rows.astype(jnp.float32), (((0,), (0,)), ((),...  18.6 us
    dot_general x8, matrix products, topic_term(): jnp.dot(ratios, word_block.astype(jnp.float32), precision=lax.Precision.H...  18 us
    dot_general x8, matrix products, ratio_block(): lax.dot_general(mix_block, word_block, (((1,), (1,)), ((), ())), preferre...  13.3 us
  transfers between devices with their start and end apart: 7, of which 5 were waited for; matrix products, arithmetic and copies ran while one was open for 7% of the time, Pallas kernels for 0%

profile of v1, /device:TPU:4, one launch (start us, length us, event | category | flops | bytes accessed | tf_op | source)
XLA Modules:
  0.0 590.3 jit_solution(16640952156614752253)
XLA Ops:
  8.6 2.5 sort.17
  13.4 11.5 %all-to-all-start = ((s32[32,1,4]{2,1,0:T(1,128)}), s32[32,1,4]{2,1,0:T(1,128)S(1)}, u32[]{:S(2)}, u32[]{:S(2)}) async-start(s32[32,1,4]{2,1,0:T(1,128)} %bitcast.1), calls=%async_computation | async-start | bytes 32768 | tf_op jit(solution)/shard_map/all_to_all | solution.py:93
  24.9 5.4 compare_select_fusion
  30.3 11.5 %gather_fusion.1 = bf16[128,16384]{1,0:T(8,128)(2,1)} fusion(bf16[128,16384]{1,0:T(8,128)(2,1)} %compare_select_fusion, s32[1024]{0:T(1024)S(1)} %pad_clamp_fusion.1), kind=kCustom, calls=%fused_computation.1 | custom fusion | bytes 8389120 | tf_op jit(solution)/shard_map/gather | solution.py:87
  41.8 7.2 %reshape.96 = bf16[32,4,16384]{2,1,0:T(4,128)(2,1)} reshape(bf16[128,16384]{1,0:T(8,128)(2,1)} %gather_fusion.1) | data formatting | bytes 8388608 | tf_op jit(solution)/shard_map/reshape | solution.py:87
  49.1 10.0 %all-to-all-start.1 = ((bf16[32,4,16384]{2,1,0:T(4,128)(2,1)}), bf16[32,4,16384]{2,1,0:T(4,128)(2,1)}, u32[]{:S(2)}, u32[]{:S(2)}) async-start(bf16[32,4,16384]{2,1,0:T(4,128)(2,1)} %reshape.96), calls=%async_computation.1 | async-start | bytes 8388608 | tf_op jit(solution)/shard_map/all_to_all | solution.py:86
  61.6 130.7 %all-to-all-done.1 = bf16[32,4,16384]{2,1,0:T(4,128)(2,1)} async-done(((bf16[32,4,16384]{2,1,0:T(4,128)(2,1)}), bf16[32,4,16384]{2,1,0:T(4,128)(2,1)}, u32[]{:S(2)}, u32[]{:S(2)}) %all-to-all-start.1) | async-done | bytes 4194336 | tf_op jit(solution)/shard_map/all_to_all | solution.py:86
  192.2 6.9 %reshape.97 = bf16[128,16384]{1,0:T(8,128)(2,1)} reshape(bf16[32,4,16384]{2,1,0:T(4,128)(2,1)} %all-to-all-done.1) | data formatting | bytes 8388608 | tf_op jit(solution)/shard_map/reshape | solution.py:92
  199.2 6.0 %broadcast_in_dim.7 = f32[16384,256]{1,0:T(8,128)} broadcast(f32[]{:T(128)} %constant.70.clone.1), dimensions={} | broadcast | bytes 16777220 | tf_op jit(solution)/shard_map/broadcast_in_dim | solution.py:69
  205.2 60.9 %while.16 = (s32[]{:T(128)}, f32[128,256]{1,0:T(8,128)S(1)}, f32[16384,256]{1,0:T(8,128)}, bf16[128,16384]{1,0:T(8,128)(2,1)}, bf16[16384,256]{1,0:T(8,128)(2,1)...) while((s32[]{:T(128)}, f32[128,256]{1,0:T(8,128)S(1)}, ...), condition=%wide.region_2.3_spmd.clone, body=%wide.region_1.2_spmd.clone.sunk | while | flops 1745420288 | bytes 10354869 | solution.py:65
  208.2 2.3 convolution_add_fusion.2
  210.4 2.3 convolution_dynamic-update-slice_fusion.2
  215.8 2.3 convolution_add_fusion.2
  218.1 2.3 convolution_dynamic-update-slice_fusion.2
  223.4 2.3 convolution_add_fusion.2
  225.6 2.3 convolution_dynamic-update-slice_fusion.2
  231.0 2.3 convolution_add_fusion.2
  233.2 2.3 convolution_dynamic-update-slice_fusion.2
  236.9 1.7 fusion.31
  238.6 2.3 convolution_add_fusion.2
  240.9 2.4 convolution_dynamic-update-slice_fusion.2
  246.3 2.3 convolution_add_fusion.2
  248.5 2.3 convolution_dynamic-update-slice_fusion.2
  253.8 2.3 convolution_add_fusion.2
  256.1 2.3 convolution_dynamic-update-slice_fusion.2
  261.5 2.3 convolution_add_fusion.2
  263.7 2.3 convolution_dynamic-update-slice_fusion.2
  269.9 4.3 collective-permute-done.1
  274.8 6.0 %collective-permute-done.2 = f32[128,256]{1,0:T(8,128)S(1)} collective-permute-done((f32[128,256]{1,0:T(8,128)S(1)}, f32[128,256]{1,0:T(8,128)S(1)}, u32[]{:S(2)}, u32[]{:S(2)}) %collective-permute-start.2) | collective-permute-done | bytes 131104 | tf_op jit(solution)/shard_map/ppermute | solution.py:13
  281.7 226.6 %reduce-scatter.2.cloned.1.call-done = f32[512,256]{1,0:T(8,128)} async-done(((f32[16384,256]{1,0:T(8,128)}), f32[512,256]{1,0:T(8,128)}) %reduce-scatter.2.cloned.1.call-update) | async-done | bytes 524304 | tf_op jit(solution)/shard_map/reduce_scatter | solution.py:71
  509.4 72.2 %psum.7 = f32[256]{0:T(256)S(1)} all-reduce(f32[256]{0:T(256)S(1)} %fusion.5), channel_id=1, replica_groups=mesh['tup'=32,'lang'=8] {'tup'}, use_global_device_ids=true, to_apply=%region_7.8 | all-reduce | flops 256 | bytes 2048 | tf_op jit(solution)/shard_map/psum | solution.py:104
  581.6 1.9 divide_bitcast_fusion
  (57 shorter events, 35.0 us)
Async XLA Ops:
  7.2 192.0 %all-gather.3.cloned.1.call-start = ((), (), s32[]{:S(2)}) async-start(), calls=%async_computation.4 | async-start | bytes 8650752 | tf_op jit(solution)/shard_map/all_gather | solution.py:49
  13.4 35.6 %all-to-all-start = ((s32[32,1,4]{2,1,0:T(1,128)}), s32[32,1,4]{2,1,0:T(1,128)S(1)}, u32[]{:S(2)}, u32[]{:S(2)}) async-start(s32[32,1,4]{2,1,0:T(1,128)} %bitcast.1), calls=%async_computation | async-start | bytes 32768 | tf_op jit(solution)/shard_map/all_to_all | solution.py:93
  49.1 11.6 %copy-start = (bf16[128,256]{1,0:T(8,128)(2,1)S(1)}, bf16[128,256]{1,0:T(8,128)(2,1)}, u32[]{:S(2)}) copy-start(bf16[128,256]{1,0:T(8,128)(2,1)} %param.10) | copy-start | bytes 196612
  49.1 143.2 %all-to-all-start.1 = ((bf16[32,4,16384]{2,1,0:T(4,128)(2,1)}), bf16[32,4,16384]{2,1,0:T(4,128)(2,1)}, u32[]{:S(2)}, u32[]{:S(2)}) async-start(bf16[32,4,16384]{2,1,0:T(4,128)(2,1)} %reshape.96), calls=%async_computation.1 | async-start | bytes 8388608 | tf_op jit(solution)/shard_map/all_to_all | solution.py:86
  59.1 449.1 %reduce-scatter.2.cloned.1.call-start = ((), (), s32[]{:S(2)}) async-start(), calls=%async_computation.3 | async-start | bytes 17301504 | tf_op jit(solution)/shard_map/reduce_scatter | solution.py:71
  266.0 242.2 %copy-start.1 = (bf16[1,512,256]{2,1,0:T(8,128)(2,1)S(1)}, bf16[1,512,256]{2,1,0:T(8,128)(2,1)}, u32[]{:S(2)}) copy-start(bf16[1,512,256]{2,1,0:T(8,128)(2,1)} %param.11) | copy-start | bytes 786436
  267.1 1.4 collective-permute-start
  268.6 5.6 collective-permute-start.1
  274.2 6.6 %collective-permute-start.2 = (f32[128,256]{1,0:T(8,128)S(1)}, f32[128,256]{1,0:T(8,128)S(1)}, u32[]{:S(2)}, u32[]{:S(2)}) collective-permute-start(f32[128,256]{1,0:T(8,128)S(1)} %add.83), channel_id=1, source_target_pairs={{0,4},{1,5},{2,6},{3,7},{4,0},{5,1},{6,2},{7,3},{8,12},{9,13},{10,... | collective-permute-start | bytes 393224 | tf_op jit(solution)/shard_map/ppermute | solution.py:13
Sparse Core Ops, SparseCore 0:
  10.6 176.9 all-gather.2
  266.2 242.0 reduce-scatter.1
